TPU v7x, 512 devices: a whole 4x4x16 slice. The times are simulated.
512 devices in a mesh: ma: 128 (over y, x, z_lo), af: 4 (over z_hi, core).
Axes of the slice: x: 4, y: 4, z: 16 (z_hi: 2, z_lo: 8; z = z_hi * 8 + z_lo), core: 2. Of those that a mesh axis runs over, the one named last changes fastest.
Arguments:
- visibilities: bfloat16 [4096, 16, 2, 2000], P('ma', 'af'), may hold values from -6 to 6
- kl_basis: bfloat16 [128, 16, 2, 2000, 128], P('ma', 'af'), may hold values from -0.109375 to 0.109375
- eigenvalues: float32 [128, 128], P('ma'), may hold values from 0.1 to 100
- kept_modes: int32 [128], P('ma'), may hold values from 32 to 128, as said below
- assigned_m: int32 [128], replicated, may hold values from 0 to 4095, as said below
Outputs:
- kl_coeffs: float32 [128, 128], P('ma')
- cleaned: float32 [128, 16, 2, 2000], P('ma', 'af')
Inputs may be any that keep to these rules, and one draw needn't show every extreme that they name: `kept_modes`: both ends are taken by some entry. `assigned_m`: 128 distinct values; 0 and 4095 are among them.
All inputs are finite; a program needn't handle non-finite values.
Results may differ from a plain program's by a relative error of at most 0.0037.
Values may be sent and summed in bfloat16 or wider, within the bound.
A program may use at most 64 MiB of HBM per device.

v0:
```python
import math

import jax
import jax.numpy as jnp
from jax import lax
from jax.sharding import PartitionSpec as P


def dft_table(assigned_m, length):
    offsets = jnp.arange(length, dtype=jnp.int32)
    phase = assigned_m[:, None] * offsets[None, :] % length
    angles = phase.astype(jnp.float32) * (2.0 * math.pi / length)
    factor = 1.0 / math.sqrt(length)
    return jnp.stack([jnp.cos(angles) * factor, -jnp.sin(angles) * factor]).astype(jnp.bfloat16)


def combine(device_parts):
    real_part = device_parts[0][..., 0, :] - device_parts[1][..., 1, :]
    imag_part = device_parts[0][..., 1, :] + device_parts[1][..., 0, :]
    return jnp.stack([real_part, imag_part], axis=-2)


def to_modes(spectra):
    return lax.all_to_all(spectra, "ma", split_axis=1, concat_axis=2, tiled=True)


def local(visibilities, kl_basis, eigenvalues, kept_modes, assigned_m):
    local_right_ascension, frequency_channels, eigen_components, baseline_pairs = visibilities.shape
    ma_count = lax.axis_size("ma")
    ra_total = local_right_ascension * ma_count
    mode_vector_width = frequency_channels * eigen_components * baseline_pairs
    piece_width = mode_vector_width // ma_count
    flattened = visibilities.reshape(local_right_ascension, ma_count, piece_width)
    dft_matrix = dft_table(assigned_m, ra_total)
    gathered = lax.all_to_all(flattened, "ma", split_axis=1, concat_axis=0, tiled=True)
    spectra = jnp.einsum(
        "smt,tk->smk", dft_matrix, gathered[:, 0, :], preferred_element_type=jnp.float32
    )
    received_pieces = to_modes(spectra[:, :, None, :])
    device_parts = received_pieces.reshape(2, frequency_channels, eigen_components, baseline_pairs)
    power_spectrum = combine(device_parts)
    rounded = power_spectrum.astype(jnp.bfloat16).reshape(1, mode_vector_width)
    matrix = kl_basis.reshape(mode_vector_width, kl_basis.shape[-1])
    partial_value = jnp.dot(rounded, matrix, preferred_element_type=jnp.float32)
    summed = lax.psum(partial_value, "af")
    keep_mask = (
        jnp.arange(matrix.shape[1], dtype=jnp.int32)[None, :] < kept_modes[:, None]
    ).astype(jnp.float32)
    gains = eigenvalues / (1.0 + eigenvalues) * keep_mask
    coeffs = summed * gains
    restored_visibilities = lax.dot_general(
        coeffs.astype(jnp.bfloat16),
        matrix,
        (((1,), (1,)), ((), ())),
        preferred_element_type=jnp.float32,
    )
    cleaned = power_spectrum[None] - restored_visibilities.reshape(
        1, frequency_channels, eigen_components, baseline_pairs
    )
    return (coeffs, cleaned)


def solution(mesh):
    in_specs = (
        P("ma", "af", None, None),
        P("ma", "af", None, None, None),
        P("ma", None),
        P("ma"),
        P(),
    )
    out_specs = (P("ma", None), P("ma", "af", None, None))
    return jax.shard_map(local, mesh=mesh, in_specs=in_specs, out_specs=out_specs, check_vma=False)
```

profile of v0, /device:TPU:1, one launch (start us, length us, event | category | flops | bytes accessed | tf_op | source)
XLA Modules:
  0.0 128.2 jit_solution(6540821703099967380)
XLA Ops:
  0.6 3.7 %reshape.157 = bf16[32,128,125]{2,1,0:T(8,128)(2,1)S(1)} reshape(bf16[32,4,2,2000]{3,2,1,0:T(2,128)(2,1)} %param.5) | data formatting | bytes 2048000 | tf_op jit(solution)/shard_map/reshape | solution.py:33
  4.3 0.0 copy-start.1
  4.3 1.7 %copy.9 = bf16[32,128,125]{2,0,1:T(8,128)(2,1)} copy(bf16[32,128,125]{2,1,0:T(8,128)(2,1)S(1)} %reshape.157) | data formatting | bytes 2048000 | tf_op jit(solution)/shard_map/reshape | solution.py:33
  6.0 20.4 %all-to-all-start = ((bf16[32,128,125]{2,0,1:T(8,128)(2,1)}), bf16[32,128,125]{2,0,1:T(8,128)(2,1)S(1)}, u32[]{:S(2)}, u32[]{:S(2)}) async-start(bf16[32,128,125]{2,0,1:T(8,128)(2,1)} %copy.9), calls=%async_computation | async-start | bytes 2097152 | tf_op jit(solution)/shard_map/all_to_all | solution.py:35
  26.4 0.0 copy-done.1
  26.4 9.1 %multiply_convert_fusion.1 = (bf16[1,128,4096]{2,1,0:T(8,128)(2,1)S(1)}, bf16[1,128,4096]{2,1,0:T(8,128)(2,1)S(1)}) fusion(s32[128]{0:T(128)S(1)} %copy-done.1), kind=kLoop, calls=%fused_computation.13 | loop fusion | flops 9961472 | bytes 2097664 | tf_op jit(solution)/shard_map/convert
  35.5 44.4 %all-to-all-done = bf16[32,128,125]{2,0,1:T(8,128)(2,1)S(1)} async-done(((bf16[32,128,125]{2,0,1:T(8,128)(2,1)}), bf16[32,128,125]{2,0,1:T(8,128)(2,1)S(1)}, u32[]{:S(2)}, u32[]{:S(2)}) %all-to-all-start) | async-done | bytes 1024032 | tf_op jit(solution)/shard_map/all_to_all | solution.py:35
  79.9 0.7 fusion.12
  80.6 0.7 copy.10
  81.3 8.4 %all-to-all-start.1 = ((f32[2,128,1,125]{3,0,2,1:T(2,128)}), f32[2,128,1,125]{3,0,2,1:T(2,128)S(1)}, u32[]{:S(2)}, u32[]{:S(2)}) async-start(f32[2,128,1,125]{3,0,2,1:T(2,128)} %copy.10), calls=%async_computation.1 | async-start | bytes 262144 | tf_op jit(solution)/shard_map/all_to_all | solution.py:24
  90.4 13.2 %all-to-all-done.1 = f32[2,128,1,125]{3,0,2,1:T(2,128)S(1)} async-done(((f32[2,128,1,125]{3,0,2,1:T(2,128)}), f32[2,128,1,125]{3,0,2,1:T(2,128)S(1)}, u32[]{:S(2)}, u32[]{:S(2)}) %all-to-all-start.1) | async-done | bytes 128032 | tf_op jit(solution)/shard_map/all_to_all | solution.py:24
  103.7 0.4 slice_reduce_fusion.1
  104.0 0.1 squeeze.8
  104.2 0.1 squeeze.7
  104.3 0.1 slice_subtract_fusion
  104.4 0.1 fusion.16
  104.5 0.1 reshape.161
  104.6 0.0 copy-start.2
  104.6 2.8 %fusion.21 = f32[1,128]{1,0:T(1,128)S(1)} fusion(bf16[16000,1]{0,1:T(2,128)(2,1)S(1)} %reshape.161, bf16[16000,128]{1,0:T(8,128)(2,1)} %bitcast.32), kind=kOutput, calls=%fused_computation.32 | convolution fusion | flops 4096000 | bytes 4128512 | tf_op jit(solution)/shard_map/dot_general | solution.py:44
  107.4 16.6 %psum.7 = f32[1,128]{1,0:T(1,128)S(1)} all-reduce(f32[1,128]{1,0:T(1,128)S(1)} %fusion.21), channel_id=1, replica_groups=mesh['ma'=128,'af'=4] {'af'}, use_global_device_ids=true, to_apply=%region_0.1 | all-reduce | flops 128 | bytes 1024 | tf_op jit(solution)/shard_map/psum | solution.py:45
  124.0 0.0 copy-done.2
  124.0 0.0 copy-start
  124.0 3.4 %fusion = f32[1,4,2,2000]{3,0,2,1:T(1,128)S(1)} fusion(bf16[1,4,2,2000,128]{4,3,2,1,0:T(8,128)(2,1)} %param.6, f32[1,128]{1,0:T(1,128)S(1)} %fusion.17), kind=kOutput, calls=%fused_computation | convolution fusion | flops 4096128 | bytes 4160512 | tf_op jit(solution)/shard_map/dot_general | solution.py:51
  127.5 0.7 fusion.15
  128.2 0.0 copy-done
  (1 shorter events, 0.0 us)
Async XLA Ops:
  4.3 22.1 %copy-start.1 = (s32[128]{0:T(128)S(1)}, s32[128]{0:T(128)}, u32[]{:S(2)}) copy-start(s32[128]{0:T(128)} %param.9) | copy-start | bytes 1540
  6.0 73.9 %all-to-all-start = ((bf16[32,128,125]{2,0,1:T(8,128)(2,1)}), bf16[32,128,125]{2,0,1:T(8,128)(2,1)S(1)}, u32[]{:S(2)}, u32[]{:S(2)}) async-start(bf16[32,128,125]{2,0,1:T(8,128)(2,1)} %copy.9), calls=%async_computation | async-start | bytes 2097152 | tf_op jit(solution)/shard_map/all_to_all | solution.py:35
  81.3 22.3 %all-to-all-start.1 = ((f32[2,128,1,125]{3,0,2,1:T(2,128)}), f32[2,128,1,125]{3,0,2,1:T(2,128)S(1)}, u32[]{:S(2)}, u32[]{:S(2)}) async-start(f32[2,128,1,125]{3,0,2,1:T(2,128)} %copy.10), calls=%async_computation.1 | async-start | bytes 262144 | tf_op jit(solution)/shard_map/all_to_all | solution.py:24
  104.6 19.4 %copy-start.2 = (f32[1,128]{1,0:T(1,128)S(1)}, f32[1,128]{1,0:T(1,128)}, u32[]{:S(2)}) copy-start(f32[1,128]{1,0:T(1,128)} %param.7) | copy-start | bytes 1540
  124.0 4.2 %copy-start = (f32[1,128]{1,0:T(1,128)}, f32[1,128]{1,0:T(1,128)S(1)}, u32[]{:S(2)}) copy-start(f32[1,128]{1,0:T(1,128)S(1)} %fusion.17) | copy-start | bytes 1540
where the time goes:
time: 130 us; the launch traced here: 128 us
  waiting for transfers between devices  57.7 us (44%)
  starting transfers between devices  28.8 us (22%)
  blocking collectives  16.6 us (13%)
  other arithmetic  9.95 us (8%)
  matrix products  6.93 us (5%)
  local copies, waits for them, and re-layouts  6.88 us (5%)
  between operations  1.39 us (1%)
    all_to_all x1, waiting for transfers between devices, local(): lax.all_to_all(flattened, 'ma', split_axis=1, concat_axis=0, tiled=True)  44.4 us
    all_to_all x1, starting transfers between devices, local(): lax.all_to_all(flattened, 'ma', split_axis=1, concat_axis=0, tiled=True)  20.4 us
    psum x1, blocking collectives, local(): summed = lax.psum(partial_value, 'af')  16.6 us
    all_to_all x1, waiting for transfers between devices, to_modes(): lax.all_to_all(spectra, 'ma', split_axis=1, concat_axis=2, tiled=True)  13.2 us
    another operation x1, other arithmetic  9.07 us
    all_to_all x1, starting transfers between devices, to_modes(): lax.all_to_all(spectra, 'ma', split_axis=1, concat_axis=2, tiled=True)  8.43 us
    reshape x2, local copies, waits for them, and re-layouts, local(): visibilities.reshape(local_right_ascension, ma_count, piece_width)  5.33 us
    dot_general x1, matrix products, local(): lax.dot_general(coeffs.astype(jnp.bfloat16), matrix, (((1,), (1,)), ((),...  3.43 us
  transfers between devices with their start and end apart: 2, of which 2 were waited for; matrix products, arithmetic and copies ran while one was open for 7% of the time, Pallas kernels for 0%

commit v1 on v0

v1 whole, which is shorter than its diff:
```python
import functools
import math

import jax
import jax.numpy as jnp
from jax import lax
from jax.experimental import pallas as pl
from jax.experimental.pallas import tpu as pltpu
from jax.sharding import PartitionSpec as P

MESH = pl.DeviceIdType.MESH
Z = 8
SIDE = 4
YX = SIDE * SIDE
LANES = 128
WIDTH = 256
AHEAD = 2
FARTHEST_FIRST = (4, 3, 5, 2, 6, 1, 7)
LEVELS = 32767.0
AHEAD = 2


def dft_block(m_column, row_shift, column_start, z, length, ra_per_device):
    rows = m_column.shape[0]
    column = lax.broadcasted_iota(jnp.int32, (rows, LANES), 1) + column_start
    part = column & 1
    per_source = 2 * ra_per_device
    source = column // per_source
    within = (column - source * per_source) >> 1
    t = source * (Z * ra_per_device) + z * ra_per_device + within
    quarter = length // 4
    phase = (m_column * t + (row_shift - part) * quarter) & (length - 1)
    wrapped = ((phase + length // 2) & (length - 1)) - length // 2
    u = quarter - jnp.abs(wrapped)
    x = u.astype(jnp.float32) * (2.0 * math.pi / length)
    x2 = x * x
    poly = jnp.float32(-1.0 / math.factorial(11))
    for order in (9, 7, 5, 3, 1):
        sign = 1.0 if order % 4 == 1 else -1.0
        poly = poly * x2 + jnp.float32(sign / math.factorial(order))
    return (x * poly * (1.0 / math.sqrt(length))).astype(jnp.bfloat16)


def kernel(
    length,
    vis,
    basis,
    eigen,
    kept,
    assigned,
    coeff_out,
    clean_out,
    recv,
    tail,
    table,
    part,
    zq,
    zs,
    zqr,
    zsr,
    fsend,
    spec,
    basis_v,
    proj,
    eigen_v,
    assigned_v,
    basis_sem,
    small_sem,
    p1_send,
    p1_recv,
    zq_send,
    zq_recv,
    zs_send,
    zs_recv,
    f_send,
    f_recv,
    a_send,
    a_recv,
    answer,
):
    chunks, _, ra, _, _ = recv.shape
    nf, _, width = vis.shape[1:]
    quarter_width = chunks * WIDTH
    tail_width = tail.shape[-1]
    per_f = YX // nf
    ma = lax.axis_index("ma")
    af = lax.axis_index("af")
    yx = ma // Z
    z = ma % Z
    y, x = yx // SIDE, yx % SIDE

    def at_yx(other):
        return (other * Z + z, af)

    def at_z(other):
        return (yx * Z + other, af)

    def peer(step):
        dy, dx = step // SIDE, step % SIDE
        return ((y + dy) % SIDE) * SIDE + (x + dx) % SIDE

    def source(step):
        dy, dx = step // SIDE, step % SIDE
        return ((y + SIDE - dy) % SIDE) * SIDE + (x + SIDE - dx) % SIDE

    basis_copy = pltpu.make_async_copy(basis, basis_v, basis_sem)
    small_copies = [
        pltpu.make_async_copy(assigned, assigned_v, small_sem.at[0]),
        pltpu.make_async_copy(eigen, eigen_v, small_sem.at[1]),
    ]
    for copy in small_copies:
        copy.start()

    barrier = pltpu.get_barrier_semaphore()
    half, core = af // 2, af % 2
    role = jnp.where(z < Z // 2, 1 - half, half)
    far = [(ma, (1 - half) * 2 + d) for d in (0, 1)]
    partners = [(ma, half * 2 + 1 - core)]
    partners += [at_z((z + d) % Z) for d in range(1, Z)]
    partners += [at_yx(peer(s)) for s in range(1, YX)]
    @pl.when(role == 1)
    def _():
        for partner in far:
            pl.semaphore_signal(barrier, inc=1, device_id=partner, device_id_type=MESH)

    for partner in partners:
        pl.semaphore_signal(barrier, inc=1, device_id=partner, device_id_type=MESH)

    def window(dest, k, wide):
        f, piece = dest // per_f, dest % per_f
        start = pl.multiple_of(piece * quarter_width + k * WIDTH, LANES)
        return vis.at[:, f, :, pl.ds(start, wide)]

    tail_start = (per_f - 1) * quarter_width + (chunks - 1) * WIDTH

    def tail_window(dest):
        return vis.at[:, dest // per_f, :, pl.ds(tail_start, tail_width)]

    is_tail = yx % per_f == per_f - 1
    for k in range(chunks):
        if k < chunks - 1:
            pltpu.make_async_copy(window(yx, k, WIDTH), recv.at[k, yx], p1_recv.at[k]).start()
        else:

            @pl.when(is_tail)
            def _():
                pltpu.make_async_copy(tail_window(yx), tail.at[yx], p1_recv.at[k]).start()

            @pl.when(jnp.logical_not(is_tail))
            def _():
                pltpu.make_async_copy(
                    window(yx, k, WIDTH), recv.at[k, yx], p1_recv.at[k]
                ).start()

    def each_piece(k, act, steps=tuple(range(1, YX))):
        for step in steps:
            if k < chunks - 1:
                act(step, k, False)
            else:
                to_tail = peer(step) % per_f == per_f - 1

                @pl.when(to_tail)
                def _():
                    act(step, k, True)

                @pl.when(jnp.logical_not(to_tail))
                def _():
                    act(step, k, False)

    @pl.when(role == 1)
    def _():
        pl.semaphore_wait(barrier, len(partners))

    @pl.when(role == 0)
    def _():
        pl.semaphore_wait(barrier, len(partners) + len(far))
        for partner in far:
            pl.semaphore_signal(answer, inc=1, device_id=partner, device_id_type=MESH)

    def p1(step, k, tailed):
        dest = peer(step)
        if tailed:
            src, dst = tail_window(dest), tail.at[yx]
        else:
            src, dst = window(dest, k, WIDTH), recv.at[k, yx]
        return pltpu.make_async_remote_copy(
            src_ref=src,
            dst_ref=dst,
            send_sem=p1_send.at[k, int(tailed)],
            recv_sem=p1_recv.at[k],
            device_id=at_yx(dest),
            device_id_type=MESH,
        )

    for k in range(min(AHEAD, chunks)):
        each_piece(k, lambda step, k, tailed: p1(step, k, tailed).start())

    basis_copy.start()

    rows = table.shape[0]
    row = lax.broadcasted_iota(jnp.int32, (rows, LANES), 0)
    lane = lax.broadcasted_iota(jnp.int32, (rows, LANES), 1)
    block = 2 * YX
    index = ((row % block) // 2) * Z + row // block
    small_copies[0].wait()
    chosen = jnp.where(lane == index, assigned_v[...].astype(jnp.float32), 0.0)
    m_column = jnp.sum(chosen, axis=1, keepdims=True).astype(jnp.int32)
    row_shift = row[:, :1] & 1
    for j in range(table.shape[1] // LANES):
        table[:, j * LANES : (j + 1) * LANES] = dft_block(
            m_column, row_shift, j * LANES, z, length, ra
        )

    def z_copies(d, k):
        target = dict(device_id=at_z((z + d) % Z), device_id_type=MESH)
        return [
            pltpu.make_async_remote_copy(
                src_ref=src.at[k, (z + d) % Z],
                dst_ref=dst.at[k, d - 1],
                send_sem=send.at[k],
                recv_sem=recv.at[k],
                **target,
            )
            for src, dst, send, recv in (
                (zs, zsr, zs_send, zs_recv),
                (zq, zqr, zq_send, zq_recv),
            )
        ]

    def rows_of(other):
        return pl.ds(pl.multiple_of(other * block, block), block)

    def arrived(ref, sem):
        pltpu.make_async_copy(ref, ref, sem).wait()

    def transform(k):
        def whole():
            arrived(recv.at[k], p1_recv.at[k])
            columns = recv[k].reshape(YX * 2 * ra, WIDTH)
            part[k] = jnp.dot(table[...], columns, preferred_element_type=jnp.float32)

        if k < chunks - 1:
            whole()
        else:

            @pl.when(is_tail)
            def _():
                arrived(tail, p1_recv.at[k])
                columns = tail[...].reshape(YX * 2 * ra, tail_width)
                part[k] = jnp.zeros_like(part[k])
                part[k, :, 0:tail_width] = jnp.dot(
                    table[...], columns, preferred_element_type=jnp.float32
                )

            @pl.when(jnp.logical_not(is_tail))
            def _():
                whole()

        pieces = part[k].reshape(Z, block, WIDTH)
        largest = jnp.maximum(jnp.max(jnp.abs(pieces), axis=1, keepdims=True), 1e-30)
        zs[k] = largest * (1.0 / LEVELS)
        zq[k] = jnp.round(pieces * (LEVELS / largest)).astype(jnp.int32).astype(jnp.int16)
        per_message = -(-(YX - 1) // (Z - 1))
        for i, d in enumerate(FARTHEST_FIRST):
            for copy in z_copies(d, k):
                copy.start()
            if k + AHEAD < chunks:
                each_piece(
                    k + AHEAD,
                    lambda step, k, tailed: p1(step, k, tailed).start(),
                    range(1, YX)[i * per_message : (i + 1) * per_message],
                )

    def place(src, k):
        start = pl.multiple_of((src % per_f) * quarter_width + k * WIDTH, LANES)
        return spec.at[src // per_f, :, pl.ds(start, WIDTH)]

    def f_local(k):
        return pltpu.make_async_copy(fsend.at[k, yx], place(yx, k), f_recv.at[k])

    def f_copy(step, k):
        dest = peer(step)
        return pltpu.make_async_remote_copy(
            src_ref=fsend.at[k, dest],
            dst_ref=place(yx, k),
            send_sem=f_send.at[k],
            recv_sem=f_recv.at[k],
            device_id=at_yx(dest),
            device_id_type=MESH,
        )

    def reduce(k):
        total = part[k, rows_of(z)]
        arrived(zsr.at[k], zs_recv.at[k])
        arrived(zqr.at[k], zq_recv.at[k])
        for d in FARTHEST_FIRST:
            total += zqr[k, d - 1].astype(jnp.float32) * zsr[k, d - 1]
        fsend[k] = total.reshape(YX, 2, WIDTH)
        f_local(k).start()
        for step in range(1, YX):
            f_copy(step, k).start()

    for k in range(chunks + 1):
        if k < chunks:
            transform(k)
        if k >= 1:
            reduce(k - 1)

    basis_copy.wait()
    total = jnp.zeros((1, LANES), jnp.float32)
    for k in range(chunks):
        arrived(fsend.at[k], f_recv.at[k])
        for piece in range(per_f):
            start = piece * quarter_width + k * WIDTH
            stop = min(start + WIDTH, width)
            for f in range(nf):
                for c in range(2):
                    rounded = spec[f, c : c + 1, start:stop].astype(jnp.bfloat16)
                    total += jnp.dot(
                        rounded, basis_v[f, c, start:stop], preferred_element_type=jnp.float32
                    )
    proj[af] = total

    def a_copy(d):
        return pltpu.make_async_remote_copy(
            src_ref=proj.at[af],
            dst_ref=proj.at[af],
            send_sem=a_send.at[d - 1],
            recv_sem=a_recv.at[d - 1],
            device_id=(ma, (af + d) % 4),
            device_id_type=MESH,
        )

    @pl.when(role == 1)
    def _():
        pl.semaphore_wait(answer, len(far))

    for d in (1, 2, 3):
        a_copy(d).start()
    for k in range(chunks):
        if k < chunks - 1:
            arrived(recv.at[k, pl.ds(0, YX - 1)], p1_send.at[k, 0])
        else:

            @pl.when(is_tail)
            def _():
                arrived(recv.at[k, pl.ds(0, YX - nf)], p1_send.at[k, 0])
                arrived(tail.at[pl.ds(0, nf - 1)], p1_send.at[k, 1])

            @pl.when(jnp.logical_not(is_tail))
            def _():
                arrived(recv.at[k, pl.ds(0, YX - nf - 1)], p1_send.at[k, 0])
                arrived(tail.at[pl.ds(0, nf)], p1_send.at[k, 1])

        arrived(zsr.at[k], zs_send.at[k])
        arrived(zqr.at[k], zq_send.at[k])
        arrived(fsend.at[k, pl.ds(0, YX - 1)], f_send.at[k])
    for d in (1, 2, 3):
        a_copy(d).wait_recv()
    summed = proj[0] + proj[1] + proj[2] + proj[3]
    lanes = lax.broadcasted_iota(jnp.int32, (1, LANES), 1)
    small_copies[1].wait()
    keep = jnp.where(lanes < kept[0], 1.0, 0.0)
    gains = eigen_v[...] / (1.0 + eigen_v[...]) * keep
    coeffs = summed * gains
    coeff_out[...] = coeffs
    half_coeffs = coeffs.astype(jnp.bfloat16)
    for f in range(nf):
        for c in range(2):
            restored = lax.dot_general(
                half_coeffs,
                basis_v[f, c],
                (((1,), (1,)), ((), ())),
                preferred_element_type=jnp.float32,
            )
            clean_out[f, c : c + 1, :] = spec[f, c : c + 1, 0:width] - restored

    for d in (1, 2, 3):
        a_copy(d).wait_send()


def local(visibilities, kl_basis, eigenvalues, kept_modes, assigned_m):
    ra, nf, _, width = visibilities.shape
    length = ra * YX * Z
    modes = kl_basis.shape[-1]
    per_f = YX // nf
    chunks = -(-width // (per_f * WIDTH))
    tail_width = width - (per_f * chunks - 1) * WIDTH
    rows = 2 * assigned_m.shape[0]
    block = 2 * YX
    f32 = jnp.float32
    dma = pltpu.SemaphoreType.DMA
    vmem, smem, hbm = pltpu.VMEM, pltpu.SMEM, pltpu.HBM
    in_hbm = functools.partial(pltpu.with_memory_space_constraint, memory_space=hbm)
    coeffs, cleaned = pl.pallas_call(
        functools.partial(kernel, length),
        out_shape=(
            vmem((1, modes), f32),
            vmem((nf, 2, width), f32),
        ),
        in_specs=[pl.BlockSpec(memory_space=s) for s in (hbm, hbm, hbm, smem, hbm)],
        out_specs=(pl.BlockSpec(memory_space=vmem), pl.BlockSpec(memory_space=vmem)),
        scratch_shapes=[
            vmem((chunks, YX, ra, 2, WIDTH), jnp.bfloat16),
            vmem((YX, ra, 2, tail_width), jnp.bfloat16),
            vmem((rows, YX * ra * 2), jnp.bfloat16),
            vmem((chunks, rows, WIDTH), f32),
            vmem((chunks, Z, block, WIDTH), jnp.int16),
            vmem((chunks, Z, 1, WIDTH), f32),
            vmem((chunks, Z - 1, block, WIDTH), jnp.int16),
            vmem((chunks, Z - 1, 1, WIDTH), f32),
            vmem((chunks, YX, 2, WIDTH), f32),
            vmem((nf, 2, per_f * chunks * WIDTH), f32),
            vmem((nf, 2, width, modes), jnp.bfloat16),
            vmem((4, 1, modes), f32),
            vmem((1, modes), f32),
            vmem((1, rows // 2), jnp.int32),
            dma,
            dma((2,)),
            dma((chunks, 2)),
            dma((chunks,)),
            dma((chunks,)),
            dma((chunks,)),
            dma((chunks,)),
            dma((chunks,)),
            dma((chunks,)),
            dma((chunks,)),
            dma((3,)),
            dma((3,)),
            pltpu.SemaphoreType.REGULAR,
        ],
        compiler_params=pltpu.CompilerParams(
            collective_id=0, has_side_effects=True, vmem_limit_bytes=40 << 20
        ),
    )(
        in_hbm(visibilities),
        in_hbm(kl_basis.reshape(nf, 2, width, modes)),
        in_hbm(eigenvalues),
        kept_modes,
        in_hbm(assigned_m.reshape(1, -1)),
    )
    return coeffs, cleaned[None]


def solution(mesh):
    in_specs = (
        P("ma", "af", None, None),
        P("ma", "af", None, None, None),
        P("ma", None),
        P("ma"),
        P(),
    )
    out_specs = (P("ma", None), P("ma", "af", None, None))
    return jax.shard_map(local, mesh=mesh, in_specs=in_specs, out_specs=out_specs, check_vma=False)
```

time: 130 us -> 55.3 us (0.43); the launches traced: 128 us -> 55.1 us
  waiting for transfers between devices: 57.7 us -> 0 us
  Pallas kernels: 0 us -> 52.7 us
  starting transfers between devices: 28.8 us -> 0 us
  blocking collectives: 16.6 us -> 0 us
  other arithmetic: 9.95 us -> 0 us
  matrix products: 6.93 us -> 0 us
  local copies, waits for them, and re-layouts: 6.88 us -> 1.14 us
    all_to_all x2 -> x0, waiting for transfers between devices: 57.7 us -> none  [the longest x1 44.4 us: local(): lax.all_to_all(flattened, 'ma', split_axis=1, concat_axis=0, tiled=True)]
    pallas_call x0 -> x1, Pallas kernels: none -> 52.7 us  [local(): pl.pallas_call(functools.partial(kernel, length), out_shape=(vmem((1, mod...]
    all_to_all x2 -> x0, starting transfers between devices: 28.8 us -> none  [the longest x1 20.4 us: local(): lax.all_to_all(flattened, 'ma', split_axis=1, concat_axis=0, tiled=True)]
    psum x1 -> x0, blocking collectives: 16.6 us -> none  [local(): summed = lax.psum(partial_value, 'af')]
    another operation x1 -> x0, other arithmetic: 9.07 us -> none
    dot_general x3 -> x0, matrix products: 6.93 us -> none  [the longest x1 3.43 us: local(): lax.dot_general(coeffs.astype(jnp.bfloat16), matrix, (((1,), (1,)), ((),...]
    reshape x2 -> x0, local copies, waits for them, and re-layouts: 5.33 us -> none  [local(): visibilities.reshape(local_right_ascension, ma_count, piece_width)]
  transfers between devices with their start and end apart: 2 -> 0, of which waited for: 2 -> 0; matrix products, arithmetic and copies ran while one was open for 7% -> 0% of each run, Pallas kernels for 0% -> 0%
where the time goes in v1:
time: 55.3 us; the launch traced here: 55.1 us
  Pallas kernels  52.7 us (95%)
  between operations  1.29 us (2%)
  local copies, waits for them, and re-layouts  1.14 us (2%)
    pallas_call x1, Pallas kernels, local(): pl.pallas_call(functools.partial(kernel, length), out_shape=(vmem((1, mod...  52.7 us
    unnamed x2, local copies, waits for them, and re-layouts  1.14 us

profile of v1, /device:TPU:1, one launch (start us, length us, event | category | flops | bytes accessed | tf_op | source)
XLA Modules:
  0.0 55.1 jit_solution(4098820997937031461)
XLA Ops:
  1.3 52.7 %shard_map.68 = (f32[1,128]{1,0:T(1,128)S(1)}, f32[4,2,2000]{2,1,0:T(2,128)S(1)}) custom-call(bf16[32,4,2,2000]{3,2,1,0:T(2,128)(2,1)} %vis.1, bf16[4,2,2000,128]{3,2,1,0:T(8,128)(2,1)} %bitcast.4, f32[1,128]{1,0:T(1,128)} %eigen.1, s32[1]{0:T(128)S(6)} %copy.11.kept, s32[1,128]{1,0:T(1,128)} %bitcast.5), custom_call_target="tpu_custom_call" | custom-call | tf_op jit(solution)/shard_map/pallas_call | solution.py:395
  54.0 0.5 copy.9
  54.5 0.6 %copy.10 = f32[1,4,2,2000]{3,2,1,0:T(2,128)} copy(f32[1,4,2,2000]{3,2,1,0:T(2,128)S(1)} %bitcast.3) | data formatting | bytes 128000

commit v2 on v1

--- a/solution.py
+++ b/solution.py
@@ -15,7 +15,7 @@
 LANES = 128
 WIDTH = 256
 AHEAD = 2
-FARTHEST_FIRST = (4, 3, 5, 2, 6, 1, 7)
+Z_STEPS = (1, 2, 3, 4, 5, 6, 7)
 LEVELS = 32767.0
 AHEAD = 2
 
@@ -61,6 +61,7 @@
     fsend,
     spec,
     basis_v,
+    basis_t,
     proj,
     eigen_v,
     assigned_v,
@@ -211,6 +212,11 @@
             m_column, row_shift, j * LANES, z, length, ra
         )
 
+    basis_copy.wait()
+    for f in range(nf):
+        for c in range(2):
+            basis_t[f, c] = basis_v[f, c].T
+
     def z_copies(d, k):
         target = dict(device_id=at_z((z + d) % Z), device_id_type=MESH)
         return [
@@ -261,7 +267,7 @@
         zs[k] = largest * (1.0 / LEVELS)
         zq[k] = jnp.round(pieces * (LEVELS / largest)).astype(jnp.int32).astype(jnp.int16)
         per_message = -(-(YX - 1) // (Z - 1))
-        for i, d in enumerate(FARTHEST_FIRST):
+        for i, d in enumerate(Z_STEPS):
             for copy in z_copies(d, k):
                 copy.start()
             if k + AHEAD < chunks:
@@ -293,7 +299,7 @@
         total = part[k, rows_of(z)]
         arrived(zsr.at[k], zs_recv.at[k])
         arrived(zqr.at[k], zq_recv.at[k])
-        for d in FARTHEST_FIRST:
+        for d in Z_STEPS:
             total += zqr[k, d - 1].astype(jnp.float32) * zsr[k, d - 1]
         fsend[k] = total.reshape(YX, 2, WIDTH)
         f_local(k).start()
@@ -306,7 +312,6 @@
         if k >= 1:
             reduce(k - 1)
 
-    basis_copy.wait()
     total = jnp.zeros((1, LANES), jnp.float32)
     for k in range(chunks):
         arrived(fsend.at[k], f_recv.at[k])
@@ -367,11 +372,8 @@
     half_coeffs = coeffs.astype(jnp.bfloat16)
     for f in range(nf):
         for c in range(2):
-            restored = lax.dot_general(
-                half_coeffs,
-                basis_v[f, c],
-                (((1,), (1,)), ((), ())),
-                preferred_element_type=jnp.float32,
+            restored = jnp.dot(
+                half_coeffs, basis_t[f, c], preferred_element_type=jnp.float32
             )
             clean_out[f, c : c + 1, :] = spec[f, c : c + 1, 0:width] - restored
 
@@ -412,6 +414,7 @@
             vmem((chunks, YX, 2, WIDTH), f32),
             vmem((nf, 2, per_f * chunks * WIDTH), f32),
             vmem((nf, 2, width, modes), jnp.bfloat16),
+            vmem((nf, 2, modes, width), jnp.bfloat16),
             vmem((4, 1, modes), f32),
             vmem((1, modes), f32),
             vmem((1, rows // 2), jnp.int32),

time: 55.3 us -> 53.7 us (0.971)
  Pallas kernels: 52.7 us -> 51.1 us
    pallas_call x1, Pallas kernels: 52.7 us -> 51.1 us  [local(): pl.pallas_call(functools.partial(kernel, length), out_shape=(vmem((1, mod...]
where the time goes in v2:
time: 53.7 us; the launch traced here: 53.5 us
  Pallas kernels  51.1 us (95%)
  between operations  1.29 us (2%)
  local copies, waits for them, and re-layouts  1.14 us (2%)
    pallas_call x1, Pallas kernels, local(): pl.pallas_call(functools.partial(kernel, length), out_shape=(vmem((1, mod...  51.1 us
    unnamed x2, local copies, waits for them, and re-layouts  1.14 us

profile of v2, /device:TPU:1, one launch (start us, length us, event | category | flops | bytes accessed | tf_op | source)
XLA Modules:
  0.0 53.5 jit_solution(4433752681653503202)
XLA Ops:
  1.3 51.1 %shard_map.68 = (f32[1,128]{1,0:T(1,128)S(1)}, f32[4,2,2000]{2,1,0:T(2,128)S(1)}) custom-call(bf16[32,4,2,2000]{3,2,1,0:T(2,128)(2,1)} %vis.1, bf16[4,2,2000,128]{3,2,1,0:T(8,128)(2,1)} %bitcast.4, f32[1,128]{1,0:T(1,128)} %eigen.1, s32[1]{0:T(128)S(6)} %copy.11.kept, s32[1,128]{1,0:T(1,128)} %bitcast.5), custom_call_target="tpu_custom_call" | custom-call | tf_op jit(solution)/shard_map/pallas_call | solution.py:397
  52.4 0.5 copy.9
  52.9 0.6 %copy.10 = f32[1,4,2,2000]{3,2,1,0:T(2,128)} copy(f32[1,4,2,2000]{3,2,1,0:T(2,128)S(1)} %bitcast.3) | data formatting | bytes 128000

commit v3 on v2

--- a/solution.py
+++ b/solution.py
@@ -114,7 +114,7 @@
 
     barrier = pltpu.get_barrier_semaphore()
     half, core = af // 2, af % 2
-    role = jnp.where(z < Z // 2, 1 - half, half)
+    role = half
     far = [(ma, (1 - half) * 2 + d) for d in (0, 1)]
     partners = [(ma, half * 2 + 1 - core)]
     partners += [at_z((z + d) % Z) for d in range(1, Z)]
@@ -340,7 +340,7 @@
     def _():
         pl.semaphore_wait(answer, len(far))
 
-    for d in (1, 2, 3):
+    for d in (2, 3, 1):
         a_copy(d).start()
     for k in range(chunks):
         if k < chunks - 1:

time: 53.7 us -> 53.7 us (level)
  no operation moved by 1% of the time
where the time goes in v3:
time: 53.7 us; the launch traced here: 53.5 us
  Pallas kernels  51.1 us (95%)
  between operations  1.29 us (2%)
  local copies, waits for them, and re-layouts  1.14 us (2%)
    pallas_call x1, Pallas kernels, local(): pl.pallas_call(functools.partial(kernel, length), out_shape=(vmem((1, mod...  51.1 us
    unnamed x2, local copies, waits for them, and re-layouts  1.14 us

profile of v3, /device:TPU:1, one launch (start us, length us, event | category | flops | bytes accessed | tf_op | source)
XLA Modules:
  0.0 53.5 jit_solution(5098535723960883770)
XLA Ops:
  1.3 51.1 %shard_map.68 = (f32[1,128]{1,0:T(1,128)S(1)}, f32[4,2,2000]{2,1,0:T(2,128)S(1)}) custom-call(bf16[32,4,2,2000]{3,2,1,0:T(2,128)(2,1)} %vis.1, bf16[4,2,2000,128]{3,2,1,0:T(8,128)(2,1)} %bitcast.4, f32[1,128]{1,0:T(1,128)} %eigen.1, s32[1]{0:T(128)S(6)} %copy.11.kept, s32[1,128]{1,0:T(1,128)} %bitcast.5), custom_call_target="tpu_custom_call" | custom-call | tf_op jit(solution)/shard_map/pallas_call | solution.py:397
  52.4 0.5 copy.9
  52.9 0.6 %copy.10 = f32[1,4,2,2000]{3,2,1,0:T(2,128)} copy(f32[1,4,2,2000]{3,2,1,0:T(2,128)S(1)} %bitcast.3) | data formatting | bytes 128000
